TPU v7x, 1024 devices: a whole 8x8x8 slice. The times are simulated.
1024 devices in a mesh: dp: 32 (over z, x_lo), ctx: 4 (over x_hi, core), tensor: 8 (over y).
Axes of the slice: x: 8 (x_hi: 2, x_lo: 4; x = x_hi * 4 + x_lo), y: 8, z: 8, core: 2. Of those that a mesh axis runs over, the one named last changes fastest.
Arguments:
- tokens: bfloat16 [20480, 7168], P(('dp', 'ctx'), 'tensor'), may hold values from -6 to 6
- routes: int32 [20480, 2], P(('dp', 'ctx')), may hold values from 0 to 31, all different within a row; in each aligned block of 160 rows (0 to 159, 160 to 319, ...) at most 12 rows name the same one
- route_weights: float32 [20480, 2], P(('dp', 'ctx')), may hold values from 0.1 to 1
- w_gate: bfloat16 [32, 7168, 1536], P('dp', 'tensor'), may hold values from -0.0625 to 0.0625
- w_up: bfloat16 [32, 7168, 1536], P('dp', 'tensor'), may hold values from -0.0625 to 0.0625
- w_down: bfloat16 [32, 1536, 7168], P('dp', None, 'tensor'), may hold values from -0.15625 to 0.15625
Outputs:
- combined: bfloat16 [20480, 7168], P(('dp', 'ctx'), 'tensor')
Inputs may be any that keep to these rules, and one draw needn't show every extreme that they name: `routes`: each row names 2 different experts; within the rows of one group of 160 tokens no expert is named by more than 12 rows, and in some groups one expert is named by exactly 12 rows.
All inputs are finite; a program needn't handle non-finite values.
Results may differ from a plain program's by a relative error of at most 0.029.
Values may be sent and summed in bfloat16 or wider, within the bound.
A program may use at most 32 MiB of HBM per device.

v0:
```python
import jax
import jax.numpy as jnp
from jax import lax
from jax.sharding import PartitionSpec as P


def rounded(values):
    narrow = lax.optimization_barrier(values.astype(jnp.bfloat16))
    return narrow.astype(jnp.float32)


def on_device(tokens, routes, route_weights, w_gate, w_up, w_down):
    expert_count = lax.axis_size("dp")
    token_count = tokens.shape[0]
    feature_count = tokens.shape[1]
    picks_count = routes.shape[1]
    capacity = token_count * picks_count * 5 // (4 * expert_count)
    expert_ids = routes.reshape(-1)
    onehot = (expert_ids[:, None] == jnp.arange(expert_count, dtype=jnp.int32)[None, :]).astype(
        jnp.int32
    )
    before = jnp.cumsum(onehot, axis=0) - onehot
    slot_index = jnp.sum(before * onehot, axis=1)
    owner_rows = jnp.arange(token_count * picks_count, dtype=jnp.int32) // picks_count
    outgoing = jnp.zeros((expert_count, capacity, feature_count), jnp.bfloat16)
    outgoing = outgoing.at[expert_ids, slot_index].set(tokens[owner_rows])
    arrived = lax.all_to_all(outgoing, "dp", split_axis=0, concat_axis=0, tiled=True)
    row_count = expert_count * capacity
    received_rows = arrived.reshape(row_count, feature_count)
    gate_part = rounded(jnp.dot(received_rows, w_gate[0], preferred_element_type=jnp.float32))
    up_part = rounded(jnp.dot(received_rows, w_up[0], preferred_element_type=jnp.float32))
    gate_sum, up_sum = (
        lax.psum(gate_part.astype(jnp.bfloat16), "tensor").astype(jnp.float32),
        lax.psum(up_part.astype(jnp.bfloat16), "tensor").astype(jnp.float32),
    )
    activated = (jax.nn.silu(gate_sum) * up_sum).astype(jnp.bfloat16)
    projected = jnp.dot(activated, w_down[0], preferred_element_type=jnp.float32)
    expert_out = projected.astype(jnp.bfloat16).reshape(expert_count, capacity, feature_count)
    returned = lax.all_to_all(expert_out, "dp", split_axis=0, concat_axis=0, tiled=True)
    picked = returned[expert_ids, slot_index].reshape(token_count, picks_count, feature_count)
    running = jnp.zeros((token_count, feature_count), jnp.float32)
    for which in range(picks_count):
        running = (
            running + picked[:, which, :].astype(jnp.float32) * route_weights[:, which][:, None]
        )
    return running.astype(jnp.bfloat16)


def solution(mesh):
    in_specs = (
        P(("dp", "ctx"), "tensor"),
        P(("dp", "ctx"), None),
        P(("dp", "ctx"), None),
        P("dp", "tensor", None),
        P("dp", "tensor", None),
        P("dp", None, "tensor"),
    )
    out_specs = P(("dp", "ctx"), "tensor")
    return jax.shard_map(
        on_device, mesh=mesh, in_specs=in_specs, out_specs=out_specs, check_vma=False
    )
```

profile of v0, /device:TPU:16, one launch (start us, length us, event | category | flops | bytes accessed | tf_op | source)
XLA Modules:
  0.0 245.0 jit_solution(11988496708920001634)
XLA Ops:
  6.5 0.9 copy.18
  7.5 0.1 eq.22
  7.6 0.1 reshape.112
  7.8 0.9 reduce-window.6
  8.7 0.2 slice_reduce_fusion
  9.0 0.1 bitcast_bitcast_fusion
  9.2 2.6 %gather_fusion = bf16[320,896]{1,0:T(8,128)(2,1)} fusion(bf16[160,896]{1,0:T(8,128)(2,1)S(1)} %copy-done.1, s32[1024]{0:T(1024)S(1)} %pad_clamp_fusion), kind=kCustom, calls=%fused_computation | custom fusion | bytes 1148160 | tf_op jit(solution)/shard_map/gather | solution.py:26
  11.8 0.1 broadcast_in_dim.2
  11.8 31.6 %scatter_fusion = bf16[32,12,896]{2,0,1:T(8,128)(2,1)S(1)} fusion(bf16[32,12,896]{2,0,1:T(8,128)(2,1)S(1)} %broadcast_in_dim.2, s32[320]{0:T(512)S(1)} %get-tuple-element.6, bf16[320,896]{1,0:T(8,128)(2,1)} %gather_fusion), kind=kCustom, calls=%fused_computation.2 | custom fusion | bytes 1722880 | tf_op jit(solution)/shard_map/scatter | solution.py:26
  43.4 0.2 copy.22
  43.6 44.5 %all_to_all.10 = bf16[32,12,896]{2,1,0:T(8,128)(2,1)} all-to-all(bf16[32,12,896]{2,1,0:T(8,128)(2,1)S(1)} %copy.22), channel_id=1, replica_groups=mesh['dp'=32,'ctx'=4,'tensor'=8] {'dp'}, dimensions={0} | all-to-all | bytes 1376256 | tf_op jit(solution)/shard_map/all_to_all | solution.py:27
  88.1 1.3 reshape.115
  89.4 2.4 convolution_convert_fusion.1
  91.8 2.4 convolution_convert_fusion
  94.3 91.5 %all-reduce.4.cloned.1.call-done = (bf16[384,1536]{1,0:T(8,128)(2,1)}, bf16[384,1536]{1,0:T(8,128)(2,1)}) async-done(((bf16[384,1536]{1,0:T(8,128)(2,1)}, bf16[384,1536]{1,0:T(8,128)(2,1)}), (bf16[384,1536]{1,0:T(8,128)(2,1)}, bf16[384,1536]{1,0:T(8,128)(2,1)})) %all-reduce.4.cloned.1.call-update) | async-done | bytes 2359312 | tf_op jit(solution)/shard_map/psum | solution.py:34
  185.8 4.0 %fusion.9 = bf16[384,896]{1,0:T(8,128)(2,1)S(1)} fusion(bf16[1,1536,896]{2,1,0:T(8,128)(2,1)} %param.11, bf16[384,1536]{1,0:T(8,128)(2,1)} %get-tuple-element.7, bf16[384,1536]{1,0:T(8,128)(2,1)} %get-tuple-element.8), kind=kOutput, calls=%fused_computation.16 | convolution fusion | flops 1062027264 | bytes 5799936 | tf_op jit(solution)/shard_map/dot_general | solution.py:37
  189.9 1.1 reshape.116
  191.0 11.2 %all-to-all-start.1 = ((bf16[32,12,896]{2,1,0:T(8,128)(2,1)}), bf16[32,12,896]{2,1,0:T(8,128)(2,1)}, u32[]{:S(2)}, u32[]{:S(2)}) async-start(bf16[32,12,896]{2,1,0:T(8,128)(2,1)} %reshape.116), calls=%async_computation.1 | async-start | bytes 1835008 | tf_op jit(solution)/shard_map/all_to_all | solution.py:39
  202.2 23.3 %all-to-all-done.1 = bf16[32,12,896]{2,1,0:T(8,128)(2,1)} async-done(((bf16[32,12,896]{2,1,0:T(8,128)(2,1)}), bf16[32,12,896]{2,1,0:T(8,128)(2,1)}, u32[]{:S(2)}, u32[]{:S(2)}) %all-to-all-start.1) | async-done | bytes 688160 | tf_op jit(solution)/shard_map/all_to_all | solution.py:39
  225.6 1.3 copy.23
  226.9 7.7 %gather_fusion.1 = bf16[320,896]{1,0:T(8,128)(2,1)} fusion(bf16[32,12,896]{2,0,1:T(8,128)(2,1)S(1)} %copy.23, s32[320]{0:T(512)S(1)} %get-tuple-element.5), kind=kCustom, calls=%fused_computation.1 | custom fusion | bytes 1149440 | tf_op jit(solution)/shard_map/gather | solution.py:40
  234.6 1.9 reshape.117
  236.5 0.8 fusion.23
  237.3 0.9 fusion.15
  (18 shorter events, 0.2 us)
Async XLA Ops:
  6.5 82.9 %copy-start = (bf16[1,896,1536]{2,1,0:T(8,128)(2,1)S(1)}, bf16[1,896,1536]{2,1,0:T(8,128)(2,1)}, u32[]{:S(2)}) copy-start(bf16[1,896,1536]{2,1,0:T(8,128)(2,1)} %param.9) | copy-start | bytes 8257540
  6.5 2.6 %copy-start.1 = (bf16[160,896]{1,0:T(8,128)(2,1)S(1)}, bf16[160,896]{1,0:T(8,128)(2,1)}, u32[]{:S(2)}) copy-start(bf16[160,896]{1,0:T(8,128)(2,1)} %param.6) | copy-start | bytes 860164
  6.5 179.3 %all-reduce.4.cloned.1.call-start = ((), (), s32[]{:S(2)}) async-start(), calls=%async_computation.2 | async-start | bytes 4718592 | tf_op jit(solution)/shard_map/psum | solution.py:34
  89.4 2.4 copy-start.3
  189.9 12.4 %copy-start.2 = (f32[160,2]{0,1:T(2,128)S(1)}, f32[160,2]{0,1:T(2,128)}, u32[]{:S(2)}) copy-start(f32[160,2]{0,1:T(2,128)} %param.8) | copy-start | bytes 3844
  191.0 34.6 %all-to-all-start.1 = ((bf16[32,12,896]{2,1,0:T(8,128)(2,1)}), bf16[32,12,896]{2,1,0:T(8,128)(2,1)}, u32[]{:S(2)}, u32[]{:S(2)}) async-start(bf16[32,12,896]{2,1,0:T(8,128)(2,1)} %reshape.116), calls=%async_computation.1 | async-start | bytes 1835008 | tf_op jit(solution)/shard_map/all_to_all | solution.py:39
Sparse Core Ops, SparseCore 0:
  94.4 91.3 all-reduce.3
where the time goes:
time: 247 us; the launch traced here: 245 us
  waiting for transfers between devices  115 us (47%)
  local copies, waits for them, and re-layouts  50 us (20%)
  blocking collectives  44.5 us (18%)
  between operations  13.6 us (6%)
  starting transfers between devices  11.2 us (5%)
  matrix products  8.83 us (4%)
    psum x1, waiting for transfers between devices, on_device(): lax.psum(up_part.astype(jnp.bfloat16), 'tensor').astype(jnp.float32)  91.5 us
    all_to_all x1, blocking collectives, on_device(): lax.all_to_all(outgoing, 'dp', split_axis=0, concat_axis=0, tiled=True)  44.5 us
    scatter x2, local copies, waits for them, and re-layouts, on_device(): outgoing = outgoing.at[expert_ids, slot_index].set(tokens[owner_rows])  31.8 us
    all_to_all x1, waiting for transfers between devices, on_device(): lax.all_to_all(expert_out, 'dp', split_axis=0, concat_axis=0, tiled=True)  23.3 us
    all_to_all x1, starting transfers between devices, on_device(): lax.all_to_all(expert_out, 'dp', split_axis=0, concat_axis=0, tiled=True)  11.2 us
    gather x1, local copies, waits for them, and re-layouts, on_device(): returned[expert_ids, slot_index]  7.71 us
  transfers between devices with their start and end apart: 2, of which 2 were waited for; matrix products, arithmetic and copies ran while one was open for 0% of the time, Pallas kernels for 0%

commit v1 on v0

v1 whole, which is shorter than its diff:
```python
import functools

import jax
import jax.numpy as jnp
from jax import lax
from jax.experimental import pallas as pl
from jax.experimental.pallas import tpu as pltpu
from jax.sharding import PartitionSpec as P

MESH = pl.DeviceIdType.MESH
BF16, F32 = jnp.bfloat16, jnp.float32

NZ, NX, NXL, NY = 8, 8, 4, 8
EXPERTS, CAP, TOK, TOPK = 32, 12, 160, 2
FEAT, HID = 896, 1536
SLOT, WIDE = 16, 768
TAIL = FEAT - WIDE
COLS = HID // 4

DZ_CHUNKS = ((1, 7), (2, 6), (3, 5), (0, 4))
NCH = len(DZ_CHUNKS)
ORDER = tuple((dz, dx) for pair in DZ_CHUNKS for dx in range(4) for dz in pair)
PER = len(ORDER) // NCH
ROWS = PER * CAP
PROWS = PER * SLOT
HALF = ROWS // 2
LAG = 2


def dot(a, b):
    return jnp.dot(a, b, preferred_element_type=F32)


def hops(c, d):
    return 4 if (c + d) % 2 == 0 else 3


def kernel(
    tok, rt, wt, wg_hbm, wu_hbm, wd_hbm, out,
    wg, wu, wd, pk, got, part, rs, act, rpk, ret, w_head, w_tail, acc,
    w_sem, d_send, d_recv, r_send, r_recv, s_send, s_recv, g_send, g_recv,
):
    dp, ctx, y = lax.axis_index("dp"), lax.axis_index("ctx"), lax.axis_index("tensor")
    z, xl = lax.div(dp, NXL), lax.rem(dp, NXL)
    xh, core = lax.div(ctx, 2), lax.rem(ctx, 2)
    x = xh * NXL + xl
    flip = lax.rem(lax.div(x, 2) + core, 2)
    x_far = lax.rem(x + NX + 2 - 4 * flip, NX)
    x_up, x_down = lax.rem(x + 1, NX), lax.rem(x + NX - 1, NX)

    def device(zz, xx):
        return (
            zz * NXL + lax.rem(xx, NXL),
            lax.div(xx, NXL) * 2 + core,
            y,
        )

    def target(dz, dx):
        return device(lax.rem(z + dz, NZ), (x, x_up, x_far, x_down)[dx])

    def source(dz, dx):
        return device(lax.rem(z + NZ - dz, NZ), (x, x_down, x_far, x_up)[dx])

    y_next = (dp, ctx, lax.rem(y + 1, NY))
    y_prev = (dp, ctx, lax.rem(y + NY - 1, NY))
    y_to = (y_next, y_prev)

    barrier = pltpu.get_barrier_semaphore()
    for dz, dx in ORDER:
        if (dz, dx) != (0, 0):
            pl.semaphore_signal(barrier, inc=1, device_id=target(dz, dx), device_id_type=MESH)
    for peer in y_to:
        pl.semaphore_signal(barrier, inc=1, device_id=peer, device_id_type=MESH)

    loads = [
        pltpu.make_async_copy(src.at[0], dst, w_sem.at[i])
        for i, (src, dst) in enumerate(((wg_hbm, wg), (wu_hbm, wu), (wd_hbm, wd)))
    ]
    for load in loads:
        load.start()

    block = lax.broadcasted_iota(jnp.int32, (EXPERTS, TOK), 0)
    expert = jnp.zeros((EXPERTS, TOK), jnp.int32)
    for p, (dz, dx) in enumerate(ORDER):
        e = lax.rem(z + dz, NZ) * NXL + lax.rem(xl + dx, NXL)
        expert = jnp.where(block == p, e, expert)
    first, second = rt[0:1, :] == expert, rt[1:2, :] == expert
    named = (first | second).astype(F32)
    earlier = (
        lax.broadcasted_iota(jnp.int32, (TOK, TOK), 0)
        < lax.broadcasted_iota(jnp.int32, (TOK, TOK), 1)
    ).astype(F32).astype(BF16)
    before = dot(named.astype(BF16), earlier)
    slot = jnp.where(first | second, before, -1.0).astype(BF16)
    weight = jnp.where(first, wt[0:1, :], jnp.where(second, wt[1:2, :], 0.0))
    weight_hi = weight.astype(BF16)
    weight_lo = (weight - weight_hi.astype(F32)).astype(BF16)
    spread = (
        lax.broadcasted_iota(jnp.int32, (EXPERTS * SLOT, EXPERTS), 0) // SLOT
        == lax.broadcasted_iota(jnp.int32, (EXPERTS * SLOT, EXPERTS), 1)
    ).astype(F32).astype(BF16)
    slots = dot(spread, slot)
    row = (lax.broadcasted_iota(jnp.int32, (EXPERTS * SLOT, TOK), 0) % SLOT).astype(F32)
    head = (slots == row) & (row < CAP)
    tails = [(slots == row - (CAP - 4 * i)) & (row >= CAP) for i in range(3)]
    pick = head.astype(F32).astype(BF16)
    picked = dot(pick, tok[:, :WIDE])
    rest = [dot(m.astype(F32).astype(BF16), tok[:, WIDE:]) for m in tails]
    for i in range(WIDE // 128):
        piece = picked[:, i * 128 : (i + 1) * 128]
        if i < 3:
            piece = piece + rest[i]
        pk[:, :, i * 128 : (i + 1) * 128] = piece.astype(BF16).reshape(EXPERTS, SLOT, 128)

    pl.semaphore_wait(barrier, len(ORDER) - 1 + len(y_to))

    for p, (dz, dx) in enumerate(ORDER):
        c = p // PER
        if (dz, dx) == (0, 0):
            pltpu.make_async_copy(pk.at[p], got.at[p], d_recv.at[c]).start()
        else:
            pltpu.make_async_remote_copy(
                src_ref=pk.at[p], dst_ref=got.at[p], send_sem=d_send.at[c], recv_sem=d_recv.at[c],
                device_id=target(dz, dx), device_id_type=MESH,
            ).start()

    heavy_hi, heavy_lo = dot(spread, weight_hi), dot(spread, weight_lo)
    for j, heavy in enumerate((heavy_hi, heavy_lo)):
        w_head[j] = jnp.where(head, heavy, 0.0).astype(BF16)
        for i in range(3):
            w_tail[j, i] = jnp.where(tails[i], heavy, 0.0).astype(BF16)
    acc[...] = jnp.zeros_like(acc)

    def places(shape, packed_axis):
        packed = lax.broadcasted_iota(jnp.int32, shape, packed_axis)
        plain = lax.broadcasted_iota(jnp.int32, shape, 1 - packed_axis)
        start, q = (packed // SLOT) * CAP, packed % SLOT
        kinds = [(plain == start + q) & (q < CAP)]
        kinds += [(plain == start + q - CAP + 4 * i) & (q >= CAP) for i in range(3)]
        return [k.astype(F32).astype(BF16) for k in kinds]

    unpack = places((ROWS, PROWS), 1)
    repack = places((PROWS, ROWS), 0)

    def owned(c, j):
        return act.at[c, pl.ds(lax.rem(j, 2) * HALF, HALF), pl.ds(pl.multiple_of(lax.div(j, 2) * COLS, COLS), COLS)]

    def owner(k, d):
        return lax.rem(y + k if d == 0 else y + NY - k, NY)

    def sum_copy(c, d, k, src):
        return pltpu.make_async_remote_copy(
            src_ref=src, dst_ref=rs.at[c, d, k - 1], send_sem=s_send.at[c, d, k - 1], recv_sem=s_recv.at[c, d, k - 1],
            device_id=y_to[d], device_id_type=MESH,
        )

    def gather_copy(c, d, k):
        piece = owned(c, owner(k - 1, 1 - d))
        return pltpu.make_async_remote_copy(
            src_ref=piece, dst_ref=piece, send_sem=g_send.at[c, d, k - 1], recv_sem=g_recv.at[c, d, k - 1],
            device_id=y_to[d], device_id_type=MESH,
        )

    def sum_src(c, d, k):
        return part.at[c, owner(hops(c, d), d)] if k == 1 else rs.at[c, d, k - 2]

    def stage_parts(c):
        span = pl.ds(c * PER, PER)
        pltpu.make_async_copy(got.at[span], got.at[span], d_recv.at[c]).wait()
        packed = got[c * PER : (c + 1) * PER].reshape(PROWS, WIDE)
        rows_head = dot(unpack[0], packed).astype(BF16)
        rows_tail = sum(dot(unpack[1 + i], packed[:, i * 128 : (i + 1) * 128]) for i in range(3)).astype(BF16)
        rows = jnp.concatenate([rows_head, rows_tail], axis=1)
        if c == 0:
            loads[0].wait()
            loads[1].wait()

        def columns(it, carry):
            cq = lax.rem(lax.div(y, 2) + 2 + it, 4)
            col = pl.ds(pl.multiple_of(cq * COLS, COLS), COLS)
            for h, w in enumerate((wg, wu)):
                sums = dot(rows, w[:, col]).astype(BF16)
                for rh in range(2):
                    part[c, 2 * cq + rh, h] = sums[rh * HALF : (rh + 1) * HALF]
            return carry

        lax.fori_loop(0, 4, columns, 0)
        for d in range(2):
            sum_copy(c, d, 1, sum_src(c, d, 1)).start()

    def stage_sum(c, k):
        for d in range(2):
            n = hops(c, d)
            if k > n:
                continue
            sum_copy(c, d, k - 1, sum_src(c, d, k - 1)).wait_recv()
            mine = part[c, owner(n - k + 1, d)].astype(F32)
            rs[c, d, k - 2] = (rs[c, d, k - 2].astype(F32) + mine).astype(BF16)
            sum_copy(c, d, k, sum_src(c, d, k)).start()

    def stage_act(c):
        total = part[c, y].astype(F32)
        for d in range(2):
            n = hops(c, d)
            sum_copy(c, d, n, sum_src(c, d, n)).wait_recv()
            total = total + rs[c, d, n - 1].astype(F32)
        gate, up = total[0], total[1]
        owned(c, y)[...] = (gate / (1.0 + jnp.exp(-gate)) * up).astype(BF16)
        for d in range(2):
            gather_copy(c, d, 1).start()

    def stage_gather(c, k):
        for d in range(2):
            if k > hops(c, d):
                continue
            gather_arrival(c, d, k - 1).wait_recv()
            gather_copy(c, d, k).start()

    def gather_arrival(c, d, k):
        piece = owned(c, owner(k, 1 - d))
        return pltpu.make_async_remote_copy(
            src_ref=piece, dst_ref=piece, send_sem=g_send.at[c, d, k - 1], recv_sem=g_recv.at[c, d, k - 1],
            device_id=y_to[d], device_id_type=MESH,
        )

    def stage_down(c):
        for d in range(2):
            gather_arrival(c, d, hops(c, d)).wait_recv()
        if c == 0:
            loads[2].wait()
        given = dot(act[c], wd[...]).astype(BF16)
        heads = dot(repack[0], given[:, :WIDE])
        for i in range(WIDE // 128):
            piece = heads[:, i * 128 : (i + 1) * 128]
            if i < 3:
                piece = piece + dot(repack[1 + i], given[:, WIDE:])
            rpk[c * PER : (c + 1) * PER, :, i * 128 : (i + 1) * 128] = piece.astype(BF16).reshape(PER, SLOT, 128)
        for p in range(c * PER, (c + 1) * PER):
            dz, dx = ORDER[p]
            if (dz, dx) == (0, 0):
                pltpu.make_async_copy(rpk.at[p], ret.at[p], r_recv.at[c]).start()
            else:
                pltpu.make_async_remote_copy(
                    src_ref=rpk.at[p], dst_ref=ret.at[p], send_sem=r_send.at[c], recv_sem=r_recv.at[c],
                    device_id=source(dz, dx), device_id_type=MESH,
                ).start()

    def stage_combine(c):
        span = pl.ds(c * PER, PER)
        pltpu.make_async_copy(ret.at[span], ret.at[span], r_recv.at[c]).wait()
        packed = ret[c * PER : (c + 1) * PER].reshape(PROWS, WIDE)
        here = slice(c * PROWS, (c + 1) * PROWS)

        def turned(weights, values):
            return lax.dot_general(weights, values, (((0,), (0,)), ((), ())), preferred_element_type=F32)

        acc[:, :WIDE] += turned(w_head[0, here], packed) + turned(w_head[1, here], packed)
        acc[:, WIDE:] += sum(
            turned(w_tail[j, i, here], packed[:, i * 128 : (i + 1) * 128]) for j in range(2) for i in range(3)
        )

    stages = (
        stage_parts,
        functools.partial(stage_sum, k=2), functools.partial(stage_sum, k=3), functools.partial(stage_sum, k=4),
        stage_act,
        functools.partial(stage_gather, k=2), functools.partial(stage_gather, k=3), functools.partial(stage_gather, k=4),
        stage_down,
    )
    for tick in range(LAG * (NCH - 1) + len(stages)):
        for c in range(NCH):
            if 0 <= tick - LAG * c < len(stages):
                stages[tick - LAG * c](c)
    for c in range(NCH):
        stage_combine(c)
    out[...] = acc[...].astype(BF16)

    for c in range(NCH):
        remote = sum(ORDER[p] != (0, 0) for p in range(c * PER, (c + 1) * PER))
        span = pl.ds(c * PER, remote)
        pltpu.make_async_copy(pk.at[span], pk.at[span], d_send.at[c]).wait()
        pltpu.make_async_copy(rpk.at[span], rpk.at[span], r_send.at[c]).wait()
        for d in range(2):
            for k in range(1, hops(c, d) + 1):
                sum_copy(c, d, k, sum_src(c, d, k)).wait_send()
                gather_copy(c, d, k).wait_send()


def on_device(tokens, routes, route_weights, w_gate, w_up, w_down):
    vmem = pl.BlockSpec(memory_space=pltpu.VMEM)
    hbm = pl.BlockSpec(memory_space=pltpu.HBM)
    dma = pltpu.SemaphoreType.DMA
    return pl.pallas_call(
        kernel,
        out_shape=jax.ShapeDtypeStruct((TOK, FEAT), BF16),
        in_specs=[vmem, vmem, vmem, hbm, hbm, hbm],
        out_specs=vmem,
        scratch_shapes=[
            pltpu.VMEM((FEAT, HID), BF16),
            pltpu.VMEM((FEAT, HID), BF16),
            pltpu.VMEM((HID, FEAT), BF16),
            pltpu.VMEM((EXPERTS, SLOT, WIDE), BF16),
            pltpu.VMEM((EXPERTS, SLOT, WIDE), BF16),
            pltpu.VMEM((NCH, NY, 2, HALF, COLS), BF16),
            pltpu.VMEM((NCH, 2, 4, 2, HALF, COLS), BF16),
            pltpu.VMEM((NCH, ROWS, HID), BF16),
            pltpu.VMEM((EXPERTS, SLOT, WIDE), BF16),
            pltpu.VMEM((EXPERTS, SLOT, WIDE), BF16),
            pltpu.VMEM((2, EXPERTS * SLOT, TOK), BF16),
            pltpu.VMEM((2, 3, EXPERTS * SLOT, TOK), BF16),
            pltpu.VMEM((TOK, FEAT), F32),
            dma((3,)),
            dma((NCH,)), dma((NCH,)), dma((NCH,)), dma((NCH,)),
            dma((NCH, 2, 4)), dma((NCH, 2, 4)), dma((NCH, 2, 4)), dma((NCH, 2, 4)),
        ],
        compiler_params=pltpu.CompilerParams(
            collective_id=0, has_side_effects=True, vmem_limit_bytes=48 * 1024 * 1024
        ),
        cost_estimate=pl.CostEstimate(flops=3_200_000_000, bytes_accessed=9_000_000, transcendentals=600_000),
    )(tokens, routes.T, route_weights.T, w_gate, w_up, w_down)


def solution(mesh):
    in_specs = (
        P(("dp", "ctx"), "tensor"),
        P(("dp", "ctx"), None),
        P(("dp", "ctx"), None),
        P("dp", "tensor", None),
        P("dp", "tensor", None),
        P("dp", None, "tensor"),
    )
    return jax.shard_map(
        on_device, mesh=mesh, in_specs=in_specs, out_specs=P(("dp", "ctx"), "tensor"), check_vma=False
    )
```

time: 247 us -> 116 us (0.47)
  the two profiles are of different devices: /device:TPU:16 before, /device:TPU:274 now
where the time goes in v1:
time: 116 us
  Pallas kernels  109 us (94%)
  local copies, waits for them, and re-layouts  6.59 us (6%)
    pallas_call x1, Pallas kernels, on_device(): pl.pallas_call(kernel, out_shape=jax.ShapeDtypeStruct((TOK, FEAT), BF16),...  109 us
    unnamed x11, local copies, waits for them, and re-layouts  6.59 us

profile of v1, /device:TPU:274, one launch (start us, length us, event | category | flops | bytes accessed | tf_op | source)
XLA Modules:
  0.0 115.8 jit_solution(4352323679844256297)
XLA Ops:
  0.0 0.0 copy-start
  0.0 1.8 %copy-done = bf16[1,896,1536]{2,1,0:T(8,128)(2,1)S(1)} copy-done((bf16[1,896,1536]{2,1,0:T(8,128)(2,1)S(1)}, bf16[1,896,1536]{2,1,0:T(8,128)(2,1)}, u32[]{:S(2)}) %copy-start) | copy-done | bytes 2752536
  1.8 0.0 copy-start.1
  1.8 1.8 %copy-done.1 = bf16[1,896,1536]{2,1,0:T(8,128)(2,1)S(1)} copy-done((bf16[1,896,1536]{2,1,0:T(8,128)(2,1)S(1)}, bf16[1,896,1536]{2,1,0:T(8,128)(2,1)}, u32[]{:S(2)}) %copy-start.1) | copy-done | bytes 2752536
  3.6 0.0 copy-start.2
  3.6 1.0 copy-done.2
  4.5 0.0 copy-start.3
  4.5 0.7 copy-done.3
  5.2 0.0 copy-start.4
  5.2 0.7 copy-done.4
  5.9 109.2 %shard_map.64 = bf16[160,896]{1,0:T(8,128)(2,1)S(1)} custom-call(bf16[160,896]{1,0:T(8,128)(2,1)S(1)} %copy-done.2, s32[2,160]{1,0:T(2,128)S(1)} %bitcast.2, f32[2,160]{1,0:T(2,128)S(1)} %bitcast.3, bf16[1,896,1536]{2,1,0:T(8,128)(2,1)S(1)} %copy-done, bf16[1,896,1536]{2,1,0:T(8,128)(2,1)S(1)} %copy-done.1, bf16[1,1536,896]{2,1,0:T(8,128)(2,1)} %wd_hbm.1), custom_call_target="tpu_custom_call" | custom-call | flops 3200000000 | bytes 9000000 | tf_op jit(solution)/shard_map/pallas_call | solution.py:292
  115.0 0.7 copy.8
Async XLA Ops:
  0.0 1.8 %copy-start = (bf16[1,896,1536]{2,1,0:T(8,128)(2,1)S(1)}, bf16[1,896,1536]{2,1,0:T(8,128)(2,1)}, u32[]{:S(2)}) copy-start(bf16[1,896,1536]{2,1,0:T(8,128)(2,1)} %wg_hbm.1) | copy-start | bytes 8257540
  1.8 1.8 %copy-start.1 = (bf16[1,896,1536]{2,1,0:T(8,128)(2,1)S(1)}, bf16[1,896,1536]{2,1,0:T(8,128)(2,1)}, u32[]{:S(2)}) copy-start(bf16[1,896,1536]{2,1,0:T(8,128)(2,1)} %wu_hbm.1) | copy-start | bytes 8257540
  3.6 1.0 copy-start.2
  4.5 0.7 copy-start.3
  5.2 0.7 copy-start.4

commit v2 on v1

--- a/solution.py
+++ b/solution.py
@@ -17,14 +17,19 @@
 TAIL = FEAT - WIDE
 COLS = HID // 4
 
-DZ_CHUNKS = ((1, 7), (2, 6), (3, 5), (0, 4))
-NCH = len(DZ_CHUNKS)
-ORDER = tuple((dz, dx) for pair in DZ_CHUNKS for dx in range(4) for dz in pair)
+CHUNKS = (
+    ((0, 0), (0, 1), (0, 2), (0, 3), (1, 0), (7, 0), (1, 1), (7, 1)),
+    ((3, 0), (5, 0), (3, 2), (5, 2), (4, 1), (4, 3), (2, 2), (6, 2)),
+    ((3, 1), (5, 1), (3, 3), (5, 3), (4, 0), (4, 2), (2, 3), (6, 3)),
+    ((1, 2), (7, 2), (1, 3), (7, 3), (2, 0), (6, 0), (2, 1), (6, 1)),
+)
+NCH = len(CHUNKS)
+ORDER = tuple(offset for chunk in CHUNKS for offset in chunk)
 PER = len(ORDER) // NCH
 ROWS = PER * CAP
 PROWS = PER * SLOT
 HALF = ROWS // 2
-LAG = 2
+LAG = 1
 
 
 def dot(a, b):
@@ -36,8 +41,8 @@
 
 
 def kernel(
-    tok, rt, wt, wg_hbm, wu_hbm, wd_hbm, out,
-    wg, wu, wd, pk, got, part, rs, act, rpk, ret, w_head, w_tail, acc,
+    tok_hbm, rt_hbm, wt_hbm, wg_hbm, wu_hbm, wd_hbm, out,
+    tok, rt, wt, wg, wu, wd, pk, got, part, rs, act, rpk, ret, w_head, w_tail, acc,
     w_sem, d_send, d_recv, r_send, r_recv, s_send, s_recv, g_send, g_recv,
 ):
     dp, ctx, y = lax.axis_index("dp"), lax.axis_index("ctx"), lax.axis_index("tensor")
@@ -65,6 +70,17 @@
     y_prev = (dp, ctx, lax.rem(y + NY - 1, NY))
     y_to = (y_next, y_prev)
 
+    inputs = [
+        pltpu.make_async_copy(src, dst, w_sem.at[3 + i])
+        for i, (src, dst) in enumerate(((rt_hbm, rt), (wt_hbm, wt), (tok_hbm, tok)))
+    ]
+    loads = [
+        pltpu.make_async_copy(src.at[0], dst, w_sem.at[i])
+        for i, (src, dst) in enumerate(((wg_hbm, wg), (wu_hbm, wu), (wd_hbm, wd)))
+    ]
+
+    for load in inputs + loads:
+        load.start()
     barrier = pltpu.get_barrier_semaphore()
     for dz, dx in ORDER:
         if (dz, dx) != (0, 0):
@@ -72,13 +88,8 @@
     for peer in y_to:
         pl.semaphore_signal(barrier, inc=1, device_id=peer, device_id_type=MESH)
 
-    loads = [
-        pltpu.make_async_copy(src.at[0], dst, w_sem.at[i])
-        for i, (src, dst) in enumerate(((wg_hbm, wg), (wu_hbm, wu), (wd_hbm, wd)))
-    ]
-    for load in loads:
-        load.start()
-
+    for load in inputs:
+        load.wait()
     block = lax.broadcasted_iota(jnp.int32, (EXPERTS, TOK), 0)
     expert = jnp.zeros((EXPERTS, TOK), jnp.int32)
     for p, (dz, dx) in enumerate(ORDER):
@@ -91,44 +102,58 @@
         < lax.broadcasted_iota(jnp.int32, (TOK, TOK), 1)
     ).astype(F32).astype(BF16)
     before = dot(named.astype(BF16), earlier)
-    slot = jnp.where(first | second, before, -1.0).astype(BF16)
+    slot = jnp.where(first | second, before, -1.0)
     weight = jnp.where(first, wt[0:1, :], jnp.where(second, wt[1:2, :], 0.0))
-    weight_hi = weight.astype(BF16)
-    weight_lo = (weight - weight_hi.astype(F32)).astype(BF16)
-    spread = (
-        lax.broadcasted_iota(jnp.int32, (EXPERTS * SLOT, EXPERTS), 0) // SLOT
-        == lax.broadcasted_iota(jnp.int32, (EXPERTS * SLOT, EXPERTS), 1)
-    ).astype(F32).astype(BF16)
-    slots = dot(spread, slot)
-    row = (lax.broadcasted_iota(jnp.int32, (EXPERTS * SLOT, TOK), 0) % SLOT).astype(F32)
-    head = (slots == row) & (row < CAP)
-    tails = [(slots == row - (CAP - 4 * i)) & (row >= CAP) for i in range(3)]
-    pick = head.astype(F32).astype(BF16)
-    picked = dot(pick, tok[:, :WIDE])
-    rest = [dot(m.astype(F32).astype(BF16), tok[:, WIDE:]) for m in tails]
-    for i in range(WIDE // 128):
-        piece = picked[:, i * 128 : (i + 1) * 128]
-        if i < 3:
-            piece = piece + rest[i]
-        pk[:, :, i * 128 : (i + 1) * 128] = piece.astype(BF16).reshape(EXPERTS, SLOT, 128)
-
+    q = lax.broadcasted_iota(jnp.int32, (PER, SLOT, TOK), 1).reshape(PROWS, TOK).astype(F32)
+    filled = {}
+
+    def repeat(values):
+        return jnp.broadcast_to(values[:, None, :], (PER, SLOT, TOK)).reshape(PROWS, TOK)
+
+    def one_hot(mask):
+        return mask.astype(F32).astype(BF16)
+
+    def stage_fill(c):
+        mine = slice(c * PER, (c + 1) * PER)
+        slots = repeat(slot[mine])
+        head = slots == q
+        tails = [(slots == q - (CAP - 4 * i)) & (q >= CAP) for i in range(3)]
+        picked = dot(one_hot(head), tok[:, :WIDE])
+        for i in range(WIDE // 128):
+            piece = picked[:, i * 128 : (i + 1) * 128]
+            if i < 3:
+                piece = piece + dot(one_hot(tails[i]), tok[:, WIDE:])
+            pk[mine, :, i * 128 : (i + 1) * 128] = piece.astype(BF16).reshape(PER, SLOT, 128)
+        filled[c] = head, tails
+
+    def stage_dispatch(c):
+        for p in range(c * PER, (c + 1) * PER):
+            dz, dx = ORDER[p]
+            if (dz, dx) == (0, 0):
+                pltpu.make_async_copy(pk.at[p], got.at[p], d_recv.at[c]).start()
+            else:
+                pltpu.make_async_remote_copy(
+                    src_ref=pk.at[p], dst_ref=got.at[p], send_sem=d_send.at[c], recv_sem=d_recv.at[c],
+                    device_id=target(dz, dx), device_id_type=MESH,
+                ).start()
+        head, tails = filled.pop(c)
+        heavy = repeat(weight[c * PER : (c + 1) * PER])
+        here = slice(c * PROWS, (c + 1) * PROWS)
+        heavy_hi = heavy.astype(BF16).astype(F32)
+        for j, part_of in enumerate((heavy_hi, heavy - heavy_hi)):
+            w_head[j, here] = jnp.where(head, part_of, 0.0).astype(BF16)
+            for i in range(3):
+                w_tail[j, i, here] = jnp.where(tails[i], part_of, 0.0).astype(BF16)
+
+    def sent(sem, ref, c):
+        remote = sum(ORDER[p] != (0, 0) for p in range(c * PER, (c + 1) * PER))
+        span = pl.ds(c * PER, remote)
+        pltpu.make_async_copy(ref.at[span], ref.at[span], sem.at[c]).wait()
+
+    stage_fill(0)
     pl.semaphore_wait(barrier, len(ORDER) - 1 + len(y_to))
-
-    for p, (dz, dx) in enumerate(ORDER):
-        c = p // PER
-        if (dz, dx) == (0, 0):
-            pltpu.make_async_copy(pk.at[p], got.at[p], d_recv.at[c]).start()
-        else:
-            pltpu.make_async_remote_copy(
-                src_ref=pk.at[p], dst_ref=got.at[p], send_sem=d_send.at[c], recv_sem=d_recv.at[c],
-                device_id=target(dz, dx), device_id_type=MESH,
-            ).start()
-
-    heavy_hi, heavy_lo = dot(spread, weight_hi), dot(spread, weight_lo)
-    for j, heavy in enumerate((heavy_hi, heavy_lo)):
-        w_head[j] = jnp.where(head, heavy, 0.0).astype(BF16)
-        for i in range(3):
-            w_tail[j, i] = jnp.where(tails[i], heavy, 0.0).astype(BF16)
+    stage_dispatch(0)
+    stage_fill(1)
     acc[...] = jnp.zeros_like(acc)
 
     def places(shape, packed_axis):
@@ -176,7 +201,7 @@
             loads[1].wait()
 
         def columns(it, carry):
-            cq = lax.rem(lax.div(y, 2) + 2 + it, 4)
+            cq = lax.rem(lax.div(y, 2) + 2 - c % 2 + it, 4)
             col = pl.ds(pl.multiple_of(cq * COLS, COLS), COLS)
             for h, w in enumerate((wg, wu)):
                 sums = dot(rows, w[:, col]).astype(BF16)
@@ -184,9 +209,10 @@
                     part[c, 2 * cq + rh, h] = sums[rh * HALF : (rh + 1) * HALF]
             return carry
 
-        lax.fori_loop(0, 4, columns, 0)
+        lax.fori_loop(0, 2, columns, 0)
         for d in range(2):
             sum_copy(c, d, 1, sum_src(c, d, 1)).start()
+        lax.fori_loop(2, 4, columns, 0)
 
     def stage_sum(c, k):
         for d in range(2):
@@ -267,18 +293,22 @@
         stage_down,
     )
     for tick in range(LAG * (NCH - 1) + len(stages)):
+        if tick < NCH - 1:
+            sent(d_send, pk, tick)
+            stage_dispatch(tick + 1)
         for c in range(NCH):
             if 0 <= tick - LAG * c < len(stages):
                 stages[tick - LAG * c](c)
+        if tick < NCH - 2:
+            stage_fill(tick + 2)
     for c in range(NCH):
         stage_combine(c)
     out[...] = acc[...].astype(BF16)
 
     for c in range(NCH):
-        remote = sum(ORDER[p] != (0, 0) for p in range(c * PER, (c + 1) * PER))
-        span = pl.ds(c * PER, remote)
-        pltpu.make_async_copy(pk.at[span], pk.at[span], d_send.at[c]).wait()
-        pltpu.make_async_copy(rpk.at[span], rpk.at[span], r_send.at[c]).wait()
+        if c == NCH - 1:
+            sent(d_send, pk, c)
+        sent(r_send, rpk, c)
         for d in range(2):
             for k in range(1, hops(c, d) + 1):
                 sum_copy(c, d, k, sum_src(c, d, k)).wait_send()
@@ -292,9 +322,12 @@
     return pl.pallas_call(
         kernel,
         out_shape=jax.ShapeDtypeStruct((TOK, FEAT), BF16),
-        in_specs=[vmem, vmem, vmem, hbm, hbm, hbm],
+        in_specs=[hbm] * 6,
         out_specs=vmem,
         scratch_shapes=[
+            pltpu.VMEM((TOK, FEAT), BF16),
+            pltpu.VMEM((TOPK, TOK), jnp.int32),
+            pltpu.VMEM((TOPK, TOK), F32),
             pltpu.VMEM((FEAT, HID), BF16),
             pltpu.VMEM((FEAT, HID), BF16),
             pltpu.VMEM((HID, FEAT), BF16),
@@ -308,12 +341,12 @@
             pltpu.VMEM((2, EXPERTS * SLOT, TOK), BF16),
             pltpu.VMEM((2, 3, EXPERTS * SLOT, TOK), BF16),
             pltpu.VMEM((TOK, FEAT), F32),
-            dma((3,)),
+            dma((6,)),
             dma((NCH,)), dma((NCH,)), dma((NCH,)), dma((NCH,)),
             dma((NCH, 2, 4)), dma((NCH, 2, 4)), dma((NCH, 2, 4)), dma((NCH, 2, 4)),
         ],
         compiler_params=pltpu.CompilerParams(
-            collective_id=0, has_side_effects=True, vmem_limit_bytes=48 * 1024 * 1024
+            collective_id=0, has_side_effects=True, vmem_limit_bytes=60 * 1024 * 1024
         ),
         cost_estimate=pl.CostEstimate(flops=3_200_000_000, bytes_accessed=9_000_000, transcendentals=600_000),
     )(tokens, routes.T, route_weights.T, w_gate, w_up, w_down)

time: 116 us -> 96.6 us (0.83)
  the two profiles are of different devices: /device:TPU:274 before, /device:TPU:18 now
where the time goes in v2:
time: 96.6 us; the launch traced here: 96.4 us
  Pallas kernels  94.7 us (98%)
  local copies, waits for them, and re-layouts  1.69 us (2%)
    pallas_call x1, Pallas kernels, on_device(): pl.pallas_call(kernel, out_shape=jax.ShapeDtypeStruct((TOK, FEAT), BF16),...  94.7 us

profile of v2, /device:TPU:18, one launch (start us, length us, event | category | flops | bytes accessed | tf_op | source)
XLA Modules:
  0.0 96.4 jit_solution(399646126360598736)
XLA Ops:
  0.0 94.7 %shard_map.64 = bf16[160,896]{1,0:T(8,128)(2,1)} custom-call(bf16[160,896]{1,0:T(8,128)(2,1)} %tok_hbm.1, s32[2,160]{1,0:T(2,128)} %bitcast.2, f32[2,160]{1,0:T(2,128)} %bitcast.3, bf16[1,896,1536]{2,1,0:T(8,128)(2,1)} %wg_hbm.1, bf16[1,896,1536]{2,1,0:T(8,128)(2,1)} %wu_hbm.1, bf16[1,1536,896]{2,1,0:T(8,128)(2,1)} %wd_hbm.1), custom_call_target="tpu_custom_call" | custom-call | flops 3200000000 | bytes 9000000 | tf_op jit(solution)/shard_map/pallas_call | solution.py:322
  94.7 1.7 %copy.8 = bf16[160,896]{1,0:T(8,128)(2,1)} copy(bf16[160,896]{1,0:T(8,128)(2,1)} %shard_map.64) | data formatting | bytes 573440

commit v3 on v2

--- a/solution.py
+++ b/solution.py
@@ -19,9 +19,9 @@
 
 CHUNKS = (
     ((0, 0), (0, 1), (0, 2), (0, 3), (1, 0), (7, 0), (1, 1), (7, 1)),
-    ((3, 0), (5, 0), (3, 2), (5, 2), (4, 1), (4, 3), (2, 2), (6, 2)),
-    ((3, 1), (5, 1), (3, 3), (5, 3), (4, 0), (4, 2), (2, 3), (6, 3)),
-    ((1, 2), (7, 2), (1, 3), (7, 3), (2, 0), (6, 0), (2, 1), (6, 1)),
+    ((4, 1), (4, 3), (3, 2), (5, 2), (3, 0), (5, 0), (2, 2), (6, 2)),
+    ((4, 2), (4, 0), (3, 3), (5, 3), (3, 1), (5, 1), (2, 3), (6, 3)),
+    ((2, 0), (6, 0), (2, 1), (6, 1), (1, 2), (7, 2), (1, 3), (7, 3)),
 )
 NCH = len(CHUNKS)
 ORDER = tuple(offset for chunk in CHUNKS for offset in chunk)
@@ -29,7 +29,7 @@
 ROWS = PER * CAP
 PROWS = PER * SLOT
 HALF = ROWS // 2
-LAG = 1
+START = (0, 1, 3, 3)
 
 
 def dot(a, b):
@@ -49,6 +49,7 @@
     z, xl = lax.div(dp, NXL), lax.rem(dp, NXL)
     xh, core = lax.div(ctx, 2), lax.rem(ctx, 2)
     x = xh * NXL + xl
+    turn = 1 - 2 * core
     flip = lax.rem(lax.div(x, 2) + core, 2)
     x_far = lax.rem(x + NX + 2 - 4 * flip, NX)
     x_up, x_down = lax.rem(x + 1, NX), lax.rem(x + NX - 1, NX)
@@ -66,9 +67,14 @@
     def source(dz, dx):
         return device(lax.rem(z + NZ - dz, NZ), (x, x_down, x_far, x_up)[dx])
 
-    y_next = (dp, ctx, lax.rem(y + 1, NY))
-    y_prev = (dp, ctx, lax.rem(y + NY - 1, NY))
-    y_to = (y_next, y_prev)
+    y_others = [(dp, ctx, lax.rem(y + k, NY)) for k in (1, NY - 1)]
+
+    barrier = pltpu.get_barrier_semaphore()
+    for dz, dx in sorted(ORDER, key=lambda o: -min(o[0], NZ - o[0]) - min(o[1], NXL - o[1])):
+        if (dz, dx) != (0, 0):
+            pl.semaphore_signal(barrier, inc=1, device_id=target(dz, dx), device_id_type=MESH)
+    for peer in y_others:
+        pl.semaphore_signal(barrier, inc=1, device_id=peer, device_id_type=MESH)
 
     inputs = [
         pltpu.make_async_copy(src, dst, w_sem.at[3 + i])
@@ -81,13 +87,6 @@
 
     for load in inputs + loads:
         load.start()
-    barrier = pltpu.get_barrier_semaphore()
-    for dz, dx in ORDER:
-        if (dz, dx) != (0, 0):
-            pl.semaphore_signal(barrier, inc=1, device_id=target(dz, dx), device_id_type=MESH)
-    for peer in y_to:
-        pl.semaphore_signal(barrier, inc=1, device_id=peer, device_id_type=MESH)
-
     for load in inputs:
         load.wait()
     block = lax.broadcasted_iota(jnp.int32, (EXPERTS, TOK), 0)
@@ -105,26 +104,26 @@
     slot = jnp.where(first | second, before, -1.0)
     weight = jnp.where(first, wt[0:1, :], jnp.where(second, wt[1:2, :], 0.0))
     q = lax.broadcasted_iota(jnp.int32, (PER, SLOT, TOK), 1).reshape(PROWS, TOK).astype(F32)
-    filled = {}
 
     def repeat(values):
         return jnp.broadcast_to(values[:, None, :], (PER, SLOT, TOK)).reshape(PROWS, TOK)
 
+    def masks(c):
+        slots = repeat(slot[c * PER : (c + 1) * PER])
+        return slots == q, [(slots == q - (CAP - 4 * i)) & (q >= CAP) for i in range(3)]
+
     def one_hot(mask):
         return mask.astype(F32).astype(BF16)
 
     def stage_fill(c):
         mine = slice(c * PER, (c + 1) * PER)
-        slots = repeat(slot[mine])
-        head = slots == q
-        tails = [(slots == q - (CAP - 4 * i)) & (q >= CAP) for i in range(3)]
+        head, tails = masks(c)
         picked = dot(one_hot(head), tok[:, :WIDE])
         for i in range(WIDE // 128):
             piece = picked[:, i * 128 : (i + 1) * 128]
             if i < 3:
                 piece = piece + dot(one_hot(tails[i]), tok[:, WIDE:])
             pk[mine, :, i * 128 : (i + 1) * 128] = piece.astype(BF16).reshape(PER, SLOT, 128)
-        filled[c] = head, tails
 
     def stage_dispatch(c):
         for p in range(c * PER, (c + 1) * PER):
@@ -136,7 +135,9 @@
                     src_ref=pk.at[p], dst_ref=got.at[p], send_sem=d_send.at[c], recv_sem=d_recv.at[c],
                     device_id=target(dz, dx), device_id_type=MESH,
                 ).start()
-        head, tails = filled.pop(c)
+
+    def stage_weights(c):
+        head, tails = masks(c)
         heavy = repeat(weight[c * PER : (c + 1) * PER])
         here = slice(c * PROWS, (c + 1) * PROWS)
         heavy_hi = heavy.astype(BF16).astype(F32)
@@ -151,10 +152,13 @@
         pltpu.make_async_copy(ref.at[span], ref.at[span], sem.at[c]).wait()
 
     stage_fill(0)
-    pl.semaphore_wait(barrier, len(ORDER) - 1 + len(y_to))
+    stage_fill(1)
+    pl.semaphore_wait(barrier, len(ORDER) - 1 + len(y_others))
     stage_dispatch(0)
-    stage_fill(1)
-    acc[...] = jnp.zeros_like(acc)
+    sent(d_send, pk, 0)
+    stage_dispatch(1)
+    for c in range(2, NCH):
+        stage_fill(c)
 
     def places(shape, packed_axis):
         packed = lax.broadcasted_iota(jnp.int32, shape, packed_axis)
@@ -168,10 +172,12 @@
     repack = places((PROWS, ROWS), 0)
 
     def owned(c, j):
-        return act.at[c, pl.ds(lax.rem(j, 2) * HALF, HALF), pl.ds(pl.multiple_of(lax.div(j, 2) * COLS, COLS), COLS)]
+        return act.at[c, j]
 
     def owner(k, d):
-        return lax.rem(y + k if d == 0 else y + NY - k, NY)
+        return lax.rem(y + NY + turn * (k if d == 0 else -k), NY)
+
+    y_to = [(dp, ctx, owner(1, d)) for d in range(2)]
 
     def sum_copy(c, d, k, src):
         return pltpu.make_async_remote_copy(
@@ -190,6 +196,10 @@
         return part.at[c, owner(hops(c, d), d)] if k == 1 else rs.at[c, d, k - 2]
 
     def stage_parts(c):
+        if c == 1:
+            sent(d_send, pk, 1)
+            for later in range(2, NCH):
+                stage_dispatch(later)
         span = pl.ds(c * PER, PER)
         pltpu.make_async_copy(got.at[span], got.at[span], d_recv.at[c]).wait()
         packed = got[c * PER : (c + 1) * PER].reshape(PROWS, WIDE)
@@ -201,7 +211,7 @@
             loads[1].wait()
 
         def columns(it, carry):
-            cq = lax.rem(lax.div(y, 2) + 2 - c % 2 + it, 4)
+            cq = lax.rem(lax.div(y, 2) + 1 + lax.rem(y, 2) + it, 4)
             col = pl.ds(pl.multiple_of(cq * COLS, COLS), COLS)
             for h, w in enumerate((wg, wu)):
                 sums = dot(rows, w[:, col]).astype(BF16)
@@ -254,7 +264,8 @@
             gather_arrival(c, d, hops(c, d)).wait_recv()
         if c == 0:
             loads[2].wait()
-        given = dot(act[c], wd[...]).astype(BF16)
+        hidden = jnp.concatenate([act[c, j : j + 2].reshape(ROWS, COLS) for j in range(0, NY, 2)], axis=1)
+        given = dot(hidden, wd[...]).astype(BF16)
         heads = dot(repack[0], given[:, :WIDE])
         for i in range(WIDE // 128):
             piece = heads[:, i * 128 : (i + 1) * 128]
@@ -292,21 +303,20 @@
         functools.partial(stage_gather, k=2), functools.partial(stage_gather, k=3), functools.partial(stage_gather, k=4),
         stage_down,
     )
-    for tick in range(LAG * (NCH - 1) + len(stages)):
-        if tick < NCH - 1:
-            sent(d_send, pk, tick)
-            stage_dispatch(tick + 1)
+    for tick in range(max(START) + len(stages)):
         for c in range(NCH):
-            if 0 <= tick - LAG * c < len(stages):
-                stages[tick - LAG * c](c)
-        if tick < NCH - 2:
-            stage_fill(tick + 2)
+            i = tick - START[c]
+            if 0 <= i < len(stages):
+                stages[i](c)
+    for c in range(NCH):
+        stage_weights(c)
+    acc[...] = jnp.zeros_like(acc)
     for c in range(NCH):
         stage_combine(c)
     out[...] = acc[...].astype(BF16)
 
     for c in range(NCH):
-        if c == NCH - 1:
+        if c >= 2:
             sent(d_send, pk, c)
         sent(r_send, rpk, c)
         for d in range(2):
@@ -335,7 +345,7 @@
             pltpu.VMEM((EXPERTS, SLOT, WIDE), BF16),
             pltpu.VMEM((NCH, NY, 2, HALF, COLS), BF16),
             pltpu.VMEM((NCH, 2, 4, 2, HALF, COLS), BF16),
-            pltpu.VMEM((NCH, ROWS, HID), BF16),
+            pltpu.VMEM((NCH, NY, HALF, COLS), BF16),
             pltpu.VMEM((EXPERTS, SLOT, WIDE), BF16),
             pltpu.VMEM((EXPERTS, SLOT, WIDE), BF16),
             pltpu.VMEM((2, EXPERTS * SLOT, TOK), BF16),

time: 96.6 us -> 96.3 us (level)
  the two profiles are of different devices: /device:TPU:18 before, /device:TPU:2 now
where the time goes in v3:
time: 96.3 us; the launch traced here: 96.2 us
  Pallas kernels  94.5 us (98%)
  local copies, waits for them, and re-layouts  1.69 us (2%)
    pallas_call x1, Pallas kernels, on_device(): pl.pallas_call(kernel, out_shape=jax.ShapeDtypeStruct((TOK, FEAT), BF16),...  94.5 us

profile of v3, /device:TPU:2, one launch (start us, length us, event | category | flops | bytes accessed | tf_op | source)
XLA Modules:
  0.0 96.2 jit_solution(7688636516070173962)
XLA Ops:
  0.0 94.5 %shard_map.64 = bf16[160,896]{1,0:T(8,128)(2,1)} custom-call(bf16[160,896]{1,0:T(8,128)(2,1)} %tok_hbm.1, s32[2,160]{1,0:T(2,128)} %bitcast.2, f32[2,160]{1,0:T(2,128)} %bitcast.3, bf16[1,896,1536]{2,1,0:T(8,128)(2,1)} %wg_hbm.1, bf16[1,896,1536]{2,1,0:T(8,128)(2,1)} %wu_hbm.1, bf16[1,1536,896]{2,1,0:T(8,128)(2,1)} %wd_hbm.1), custom_call_target="tpu_custom_call" | custom-call | flops 3200000000 | bytes 9000000 | tf_op jit(solution)/shard_map/pallas_call | solution.py:332
  94.5 1.7 %copy.8 = bf16[160,896]{1,0:T(8,128)(2,1)} copy(bf16[160,896]{1,0:T(8,128)(2,1)} %shard_map.64) | data formatting | bytes 573440

commit v4 on v3

--- a/solution.py
+++ b/solution.py
@@ -29,7 +29,7 @@
 ROWS = PER * CAP
 PROWS = PER * SLOT
 HALF = ROWS // 2
-START = (0, 1, 3, 3)
+START = (0, 1, 2, 2)
 
 
 def dot(a, b):
@@ -69,13 +69,6 @@
 
     y_others = [(dp, ctx, lax.rem(y + k, NY)) for k in (1, NY - 1)]
 
-    barrier = pltpu.get_barrier_semaphore()
-    for dz, dx in sorted(ORDER, key=lambda o: -min(o[0], NZ - o[0]) - min(o[1], NXL - o[1])):
-        if (dz, dx) != (0, 0):
-            pl.semaphore_signal(barrier, inc=1, device_id=target(dz, dx), device_id_type=MESH)
-    for peer in y_others:
-        pl.semaphore_signal(barrier, inc=1, device_id=peer, device_id_type=MESH)
-
     inputs = [
         pltpu.make_async_copy(src, dst, w_sem.at[3 + i])
         for i, (src, dst) in enumerate(((rt_hbm, rt), (wt_hbm, wt), (tok_hbm, tok)))
@@ -87,6 +80,13 @@
 
     for load in inputs + loads:
         load.start()
+    barrier = pltpu.get_barrier_semaphore()
+    for dz, dx in ORDER:
+        if (dz, dx) != (0, 0):
+            pl.semaphore_signal(barrier, inc=1, device_id=target(dz, dx), device_id_type=MESH)
+    for peer in y_others:
+        pl.semaphore_signal(barrier, inc=1, device_id=peer, device_id_type=MESH)
+
     for load in inputs:
         load.wait()
     block = lax.broadcasted_iota(jnp.int32, (EXPERTS, TOK), 0)

time: 96.3 us -> 95.4 us (level)
  Pallas kernels: 94.5 us -> 93.3 us
    pallas_call x1, Pallas kernels: 94.5 us -> 93.3 us  [on_device(): pl.pallas_call(kernel, out_shape=jax.ShapeDtypeStruct((TOK, FEAT), BF16),...]
where the time goes in v4:
time: 95.4 us; the launch traced here: 95 us
  Pallas kernels  93.3 us (98%)
  local copies, waits for them, and re-layouts  1.69 us (2%)
    pallas_call x1, Pallas kernels, on_device(): pl.pallas_call(kernel, out_shape=jax.ShapeDtypeStruct((TOK, FEAT), BF16),...  93.3 us

profile of v4, /device:TPU:2, one launch (start us, length us, event | category | flops | bytes accessed | tf_op | source)
XLA Modules:
  0.0 95.0 jit_solution(3029846207111450162)
XLA Ops:
  0.0 93.3 %shard_map.64 = bf16[160,896]{1,0:T(8,128)(2,1)} custom-call(bf16[160,896]{1,0:T(8,128)(2,1)} %tok_hbm.1, s32[2,160]{1,0:T(2,128)} %bitcast.2, f32[2,160]{1,0:T(2,128)} %bitcast.3, bf16[1,896,1536]{2,1,0:T(8,128)(2,1)} %wg_hbm.1, bf16[1,896,1536]{2,1,0:T(8,128)(2,1)} %wu_hbm.1, bf16[1,1536,896]{2,1,0:T(8,128)(2,1)} %wd_hbm.1), custom_call_target="tpu_custom_call" | custom-call | flops 3200000000 | bytes 9000000 | tf_op jit(solution)/shard_map/pallas_call | solution.py:332
  93.3 1.7 %copy.8 = bf16[160,896]{1,0:T(8,128)(2,1)} copy(bf16[160,896]{1,0:T(8,128)(2,1)} %shard_map.64) | data formatting | bytes 573440
